TPU v7x, 32 devices: a whole 2x2x4 slice. The times are simulated.
32 devices in a mesh: fsdp: 32 (over z, y, x, core).
Axes of the slice: x: 2, y: 2, z: 4, core: 2. Of those that a mesh axis runs over, the one named last changes fastest.
Arguments:
- patches: bfloat16 [2, 16384, 768], P(None, 'fsdp'), may hold values from -6 to 6
- tile_kind: int32 [64], P('fsdp'), may hold values from 0 to 2
- out_grad: bfloat16 [2, 16384, 768], P(None, 'fsdp'), may hold values from -6 to 6
- norm1_gain: bfloat16 [2, 768], P(None, 'fsdp'), may hold values from 0.25 to 1.75
- norm1_bias: bfloat16 [2, 768], P(None, 'fsdp'), may hold values from -1.75 to 1.75
- w_qkv: bfloat16 [2, 768, 2304], P(None, 'fsdp'), may hold values from -0.21875 to 0.21875
- w_proj: bfloat16 [2, 768, 768], P(None, 'fsdp'), may hold values from -1.25 to 1.25
- b_proj: bfloat16 [2, 768], P(None, 'fsdp'), may hold values from -3 to 3
- norm2_gain: bfloat16 [2, 768], P(None, 'fsdp'), may hold values from 0.25 to 1.75
- norm2_bias: bfloat16 [2, 768], P(None, 'fsdp'), may hold values from -1.75 to 1.75
- w_fc1: bfloat16 [2, 768, 3072], P(None, 'fsdp'), may hold values from -0.21875 to 0.21875
- b_fc1: bfloat16 [2, 3072], P(None, 'fsdp'), may hold values from -3 to 3
- w_fc2: bfloat16 [2, 3072, 768], P(None, 'fsdp'), may hold values from -0.109375 to 0.109375
- b_fc2: bfloat16 [2, 768], P(None, 'fsdp'), may hold values from -3 to 3
Outputs:
- encoded: bfloat16 [2, 16384, 768], P(None, 'fsdp')
- patches_grad: float32 [2, 16384, 768], P(None, 'fsdp')
- norm1_gain_grad: float32 [2, 768], P(None, 'fsdp')
- norm1_bias_grad: float32 [2, 768], P(None, 'fsdp')
- w_qkv_grad: float32 [2, 768, 2304], P(None, 'fsdp')
- w_proj_grad: float32 [2, 768, 768], P(None, 'fsdp')
- b_proj_grad: float32 [2, 768], P(None, 'fsdp')
- norm2_gain_grad: float32 [2, 768], P(None, 'fsdp')
- norm2_bias_grad: float32 [2, 768], P(None, 'fsdp')
- w_fc1_grad: float32 [2, 768, 3072], P(None, 'fsdp')
- b_fc1_grad: float32 [2, 3072], P(None, 'fsdp')
- w_fc2_grad: float32 [2, 3072, 768], P(None, 'fsdp')
- b_fc2_grad: float32 [2, 768], P(None, 'fsdp')
All inputs are finite; a program needn't handle non-finite values.
Results may differ from a plain program's by a relative error of at most 0.011.
Values may be sent and summed in bfloat16 or wider, within the bound.
A program may use at most 256 MiB of HBM per device.

v0:
```python
import jax
import jax.numpy as jnp
from jax import lax
from jax.sharding import PartitionSpec as P

HEADS = 12
SIDE_S = 12
SIDE_M = 15
SIDE_L = 20


def layer_norm(values, gain, shift):
    center = values - jnp.mean(values, axis=-1, keepdims=True)
    spread = jnp.mean(center * center, axis=-1, keepdims=True)
    return center * lax.rsqrt(spread + 1e-06) * gain + shift


def exact_gelu(values):
    return jax.nn.gelu(values, approximate=False)


def contract_rows(left, right):
    return lax.dot_general(
        left, right, (((0,), (0,)), ((), ())), preferred_element_type=jnp.float32
    )


def contract_cols(left, right):
    return lax.dot_general(
        left, right, (((1,), (1,)), ((), ())), preferred_element_type=jnp.float32
    )


def packing(kind_ids, row_count):
    slot_count = kind_ids.shape[0]
    grid_sides = jnp.where(kind_ids == 0, SIDE_S, jnp.where(kind_ids == 1, SIDE_M, SIDE_L)).astype(
        jnp.int32
    )
    lengths = grid_sides * grid_sides
    end_rows = jnp.cumsum(lengths)
    starts = end_rows - lengths
    places = jnp.arange(row_count, dtype=jnp.int32)
    fitting = end_rows <= row_count
    inside = (
        fitting[None, :]
        & (places[:, None] >= starts[None, :])
        & (places[:, None] < end_rows[None, :])
    ).astype(jnp.int32)
    filled = jnp.sum(inside, axis=1)
    slot_ids = jnp.arange(slot_count, dtype=jnp.int32)
    segment = jnp.sum(inside * slot_ids[None, :], axis=1) + (1 - filled) * (slot_count + places)
    offset = places - jnp.sum(inside * starts[None, :], axis=1)
    grid_side = jnp.sum(inside * grid_sides[None, :], axis=1) + (1 - filled)
    grid_rows = offset // grid_side
    grid_cols = offset % grid_side
    return (segment, grid_rows, grid_cols, filled)


def split_heads(qkv_rows):
    row_count = qkv_rows.shape[0]
    width = qkv_rows.shape[1] // 3
    return qkv_rows.reshape(row_count, 3, HEADS, width // HEADS)


def block_logits(query_rows, keys_all, layout):
    segment, grid_rows, grid_cols = layout
    head_size = keys_all.shape[2]
    row_gap = (grid_rows[:, None] - grid_rows[None, :]).astype(jnp.float32)
    col_gap = (grid_cols[:, None] - grid_cols[None, :]).astype(jnp.float32)
    distance = jnp.sqrt(row_gap * row_gap + col_gap * col_gap)
    slopes = jnp.exp2(-8.0 * (jnp.arange(HEADS, dtype=jnp.float32) + 1.0) / HEADS)
    logits = (
        jnp.einsum("qhd,khd->hqk", query_rows, keys_all, preferred_element_type=jnp.float32)
        * head_size ** (-0.5)
        - slopes[:, None, None] * distance[None]
    )
    same_sample = segment[:, None] == segment[None, :]
    return jnp.where(same_sample[None], logits, -1e30)


def attend(qkv_rows, layout):
    row_count = qkv_rows.shape[0]
    parts = split_heads(qkv_rows)
    queries, keys_all, values_all = (parts[:, 0], parts[:, 1], parts[:, 2])
    block_rows = min(512, row_count)

    def one_block(block_index):
        masked = block_logits(queries, keys_all, layout)
        highest = jnp.max(masked, axis=-1, keepdims=True)
        unnormed = jnp.exp(masked - highest)
        totals = jnp.sum(unnormed, axis=-1, keepdims=True)
        probability = (unnormed / totals).astype(jnp.bfloat16)
        mixed = jnp.einsum(
            "hqk,khd->qhd", probability, values_all, preferred_element_type=jnp.float32
        )
        return (mixed.astype(jnp.bfloat16), (highest + jnp.log(totals))[:, :, 0])

    mixed, log_totals = lax.map(one_block, jnp.arange(row_count // block_rows))
    return (mixed.reshape(row_count, -1), log_totals)


def attend_back(qkv_rows, log_totals, mixed_grad, layout):
    row_count = qkv_rows.shape[0]
    parts = split_heads(qkv_rows)
    queries, keys_all, values_all = (parts[:, 0], parts[:, 1], parts[:, 2])
    head_size = parts.shape[3]
    scale = head_size ** (-0.5)
    grad_heads = mixed_grad.reshape(row_count, HEADS, head_size)
    block_rows = min(512, row_count)

    def one_block(carry, inputs):
        key_grad, value_grad = carry
        block_index, block_totals = inputs
        masked = block_logits(queries, keys_all, layout)
        probability = jnp.exp(masked - block_totals[:, :, None])
        value_grad = value_grad + jnp.einsum(
            "hqk,qhd->khd",
            probability.astype(jnp.bfloat16),
            grad_heads,
            preferred_element_type=jnp.float32,
        )
        prob_grad = jnp.einsum(
            "qhd,khd->hqk", grad_heads, values_all, preferred_element_type=jnp.float32
        )
        centered = jnp.sum(probability * prob_grad, axis=-1, keepdims=True)
        logit_grad = (probability * (prob_grad - centered)).astype(jnp.bfloat16)
        query_grad = (
            jnp.einsum("hqk,khd->qhd", logit_grad, keys_all, preferred_element_type=jnp.float32)
            * scale
        )
        key_grad = (
            key_grad
            + jnp.einsum("hqk,qhd->khd", logit_grad, queries, preferred_element_type=jnp.float32)
            * scale
        )
        return ((key_grad, value_grad), query_grad)

    zero_heads = jnp.zeros((row_count, HEADS, head_size), jnp.float32)
    block_ids = jnp.arange(row_count // block_rows)
    (key_grad, value_grad), query_grad = lax.scan(
        one_block, (zero_heads, zero_heads), (block_ids, log_totals)
    )
    stacked = jnp.stack(
        [query_grad.reshape(row_count, HEADS, head_size), key_grad, value_grad], axis=1
    )
    return stacked.reshape(row_count, -1).astype(jnp.bfloat16)


def encode_forward(weights, tokens_in, layout):
    gain_a, shift_a, w_attn, w_out, bias_out, gain_b, shift_b, w_up, bias_up, w_down, bias_down = (
        weights
    )
    inputs_f = tokens_in.astype(jnp.float32)
    normed = layer_norm(inputs_f, gain_a.astype(jnp.float32), shift_a.astype(jnp.float32)).astype(
        jnp.bfloat16
    )
    qkv_rows = jnp.dot(normed, w_attn, preferred_element_type=jnp.float32).astype(jnp.bfloat16)
    mixed, log_totals = attend(qkv_rows, layout)
    first = inputs_f + (
        jnp.dot(mixed, w_out, preferred_element_type=jnp.float32) + bias_out.astype(jnp.float32)
    )
    normed_b = layer_norm(first, gain_b.astype(jnp.float32), shift_b.astype(jnp.float32)).astype(
        jnp.bfloat16
    )
    hidden = jnp.dot(normed_b, w_up, preferred_element_type=jnp.float32) + bias_up.astype(
        jnp.float32
    )
    active = exact_gelu(hidden).astype(jnp.bfloat16)
    result = first + (
        jnp.dot(active, w_down, preferred_element_type=jnp.float32) + bias_down.astype(jnp.float32)
    )
    return (
        result,
        (inputs_f, normed, qkv_rows, mixed, log_totals, first, normed_b, hidden, active),
    )


def encode_backward(weights, tokens_in, layout, cotangent):
    gain_a, shift_a, w_attn, w_out, bias_out, gain_b, shift_b, w_up, bias_up, w_down, bias_down = (
        weights
    )
    _result, saved = encode_forward(weights, tokens_in, layout)
    inputs_f, normed, qkv_rows, mixed, log_totals, first, normed_b, hidden, active = saved
    down_grad = cotangent.astype(jnp.bfloat16)
    grad_w_down = contract_rows(active, down_grad)
    grad_bias_down = jnp.sum(down_grad.astype(jnp.float32), axis=0)
    active_grad = contract_cols(down_grad, w_down)
    _hidden_out, gelu_back = jax.vjp(exact_gelu, hidden)
    hidden_grad = gelu_back(active_grad)[0].astype(jnp.bfloat16)
    grad_w_up = contract_rows(normed_b, hidden_grad)
    grad_bias_up = jnp.sum(hidden_grad.astype(jnp.float32), axis=0)
    normed_b_grad = contract_cols(hidden_grad, w_up)
    _norm_out, norm_back = jax.vjp(
        layer_norm, first, gain_b.astype(jnp.float32), shift_b.astype(jnp.float32)
    )
    first_part, grad_gain_b, grad_shift_b = norm_back(normed_b_grad)
    first_grad = cotangent + first_part
    branch_grad = first_grad.astype(jnp.bfloat16)
    grad_w_out = contract_rows(mixed, branch_grad)
    grad_bias_out = jnp.sum(branch_grad.astype(jnp.float32), axis=0)
    mixed_grad = contract_cols(branch_grad, w_out).astype(jnp.bfloat16)
    qkv_grad = attend_back(qkv_rows, log_totals, mixed_grad, layout)
    grad_w_attn = contract_rows(normed, qkv_grad)
    normed_grad = contract_cols(qkv_grad, w_attn)
    _first_out, norm_back_a = jax.vjp(
        layer_norm, inputs_f, gain_a.astype(jnp.float32), shift_a.astype(jnp.float32)
    )
    input_part, grad_gain_a, grad_shift_a = norm_back_a(normed_grad)
    return (
        first_grad + input_part,
        (
            grad_gain_a,
            grad_shift_a,
            grad_w_attn,
            grad_w_out,
            grad_bias_out,
            grad_gain_b,
            grad_shift_b,
            grad_w_up,
            grad_bias_up,
            grad_w_down,
            grad_bias_down,
        ),
    )


def local(
    patches,
    tile_kind,
    out_grad,
    norm1_gain,
    norm1_bias,
    w_qkv,
    w_proj,
    b_proj,
    norm2_gain,
    norm2_bias,
    w_fc1,
    b_fc1,
    w_fc2,
    b_fc2,
):
    row_count = patches.shape[1]
    segment, grid_rows, grid_cols, filled = packing(tile_kind, row_count)
    layout = (segment, grid_rows, grid_cols)
    live_rows = filled.astype(jnp.float32)[:, None]
    encoded_list = []
    gathered = []
    for modality in range(2):
        weights = (
            lax.all_gather(norm1_gain[modality], "fsdp", axis=0, tiled=True),
            lax.all_gather(norm1_bias[modality], "fsdp", axis=0, tiled=True),
            lax.all_gather(w_qkv[modality], "fsdp", axis=0, tiled=True),
            lax.all_gather(w_proj[modality], "fsdp", axis=0, tiled=True),
            lax.all_gather(b_proj[modality], "fsdp", axis=0, tiled=True),
            lax.all_gather(norm2_gain[modality], "fsdp", axis=0, tiled=True),
            lax.all_gather(norm2_bias[modality], "fsdp", axis=0, tiled=True),
            lax.all_gather(w_fc1[modality], "fsdp", axis=0, tiled=True),
            lax.all_gather(b_fc1[modality], "fsdp", axis=0, tiled=True),
            lax.all_gather(w_fc2[modality], "fsdp", axis=0, tiled=True),
            lax.all_gather(b_fc2[modality], "fsdp", axis=0, tiled=True),
        )
        result, _saved = encode_forward(weights, patches[modality], layout)
        encoded_list.append(result.astype(jnp.bfloat16))
        gathered.append(weights)
    input_grads = []
    block_shares = []
    for modality in range(2):
        weights = (
            lax.all_gather(norm1_gain[modality], "fsdp", axis=0, tiled=True),
            lax.all_gather(norm1_bias[modality], "fsdp", axis=0, tiled=True),
            lax.all_gather(w_qkv[modality], "fsdp", axis=0, tiled=True),
            lax.all_gather(w_proj[modality], "fsdp", axis=0, tiled=True),
            lax.all_gather(b_proj[modality], "fsdp", axis=0, tiled=True),
            lax.all_gather(norm2_gain[modality], "fsdp", axis=0, tiled=True),
            lax.all_gather(norm2_bias[modality], "fsdp", axis=0, tiled=True),
            lax.all_gather(w_fc1[modality], "fsdp", axis=0, tiled=True),
            lax.all_gather(b_fc1[modality], "fsdp", axis=0, tiled=True),
            lax.all_gather(w_fc2[modality], "fsdp", axis=0, tiled=True),
            lax.all_gather(b_fc2[modality], "fsdp", axis=0, tiled=True),
        )
        cotangent = out_grad[modality].astype(jnp.float32) * live_rows
        input_grad, weight_grads = encode_backward(weights, patches[modality], layout, cotangent)
        input_grads.append(input_grad)
        block_shares.append(
            (
                lax.psum_scatter(weight_grads[0], "fsdp", scatter_dimension=0, tiled=True),
                lax.psum_scatter(weight_grads[1], "fsdp", scatter_dimension=0, tiled=True),
                lax.psum_scatter(weight_grads[2], "fsdp", scatter_dimension=0, tiled=True),
                lax.psum_scatter(weight_grads[3], "fsdp", scatter_dimension=0, tiled=True),
                lax.psum_scatter(weight_grads[4], "fsdp", scatter_dimension=0, tiled=True),
                lax.psum_scatter(weight_grads[5], "fsdp", scatter_dimension=0, tiled=True),
                lax.psum_scatter(weight_grads[6], "fsdp", scatter_dimension=0, tiled=True),
                lax.psum_scatter(weight_grads[7], "fsdp", scatter_dimension=0, tiled=True),
                lax.psum_scatter(weight_grads[8], "fsdp", scatter_dimension=0, tiled=True),
                lax.psum_scatter(weight_grads[9], "fsdp", scatter_dimension=0, tiled=True),
                lax.psum_scatter(weight_grads[10], "fsdp", scatter_dimension=0, tiled=True),
            )
        )
    stacked = [
        jnp.stack([block_shares[0][member], block_shares[1][member]]) for member in range(11)
    ]
    return (
        jnp.stack(encoded_list),
        jnp.stack(input_grads),
        stacked[0],
        stacked[1],
        stacked[2],
        stacked[3],
        stacked[4],
        stacked[5],
        stacked[6],
        stacked[7],
        stacked[8],
        stacked[9],
        stacked[10],
    )


def solution(mesh):
    in_specs = (
        P(None, "fsdp", None),
        P("fsdp"),
        P(None, "fsdp", None),
        P(None, "fsdp"),
        P(None, "fsdp"),
        P(None, "fsdp", None),
        P(None, "fsdp", None),
        P(None, "fsdp"),
        P(None, "fsdp"),
        P(None, "fsdp"),
        P(None, "fsdp", None),
        P(None, "fsdp"),
        P(None, "fsdp", None),
        P(None, "fsdp"),
    )
    out_specs = (
        P(None, "fsdp", None),
        P(None, "fsdp", None),
        P(None, "fsdp"),
        P(None, "fsdp"),
        P(None, "fsdp", None),
        P(None, "fsdp", None),
        P(None, "fsdp"),
        P(None, "fsdp"),
        P(None, "fsdp"),
        P(None, "fsdp", None),
        P(None, "fsdp"),
        P(None, "fsdp", None),
        P(None, "fsdp"),
    )
    return jax.shard_map(local, mesh=mesh, in_specs=in_specs, out_specs=out_specs, check_vma=False)
```

profile of v0, /device:TPU:0, one launch (start us, length us, event | category | flops | bytes accessed | tf_op | source)
XLA Modules:
  0.0 1540.0 jit_solution(6909679407308099877)
XLA Ops:
  27.0 44.2 %all-reduce.29 = (bf16[768]{0:T(1024)(128)(2,1)S(1)}, bf16[768]{0:T(1024)(128)(2,1)S(1)}, bf16[768]{0:T(1024)(128)(2,1)S(1)}, bf16[768]{0:T(1024)(128)(2,1)S(1)}...) all-reduce(bf16[768]{0:T(1024)(128)(2,1)S(1)} %dynamic-update-slice, ...), channel_id=14, replica_groups=mesh['fsdp'=32] {'fsdp'}, use_global_device_ids=true, to_apply=%add.8 | all-reduce | flops 15360 | bytes 61440
  74.7 5.9 convolution_convert_fusion
  98.1 32.1 %all-gather.41.cloned.1.call-done = bf16[1,768,768]{2,1,0:T(8,128)(2,1)} async-done(((bf16[1,24,768]{2,1,0:T(8,128)(2,1)}), bf16[1,768,768]{2,1,0:T(8,128)(2,1)}) %all-gather.41.cloned.1.call-update) | async-done | bytes 1179664 | tf_op jit(solution)/shard_map/all_gather | solution.py:254
  133.6 62.7 %all-gather.43.cloned.1.call-done = bf16[1,768,3072]{2,1,0:T(8,128)(2,1)} async-done(((bf16[1,24,3072]{2,1,0:T(8,128)(2,1)}), bf16[1,768,3072]{2,1,0:T(8,128)(2,1)}) %all-gather.43.cloned.1.call-update) | async-done | bytes 4718608 | tf_op jit(solution)/shard_map/all_gather | solution.py:258
  196.4 21.0 %multiply_convert_fusion.2 = (bf16[512,3072]{1,0:T(8,128)(2,1)}, f32[512,3072]{1,0:T(8,128)}, f32[512,3072]{1,0:T(8,128)}) fusion(f32[3072]{0:T(1024)S(1)} %convert_element_type.390, bf16[1,768,3072]{2,1,0:T(8,128)(2,1)} %all-gather.43.cloned.1.call-done, f32[512,768]{1,0:T(8,128)} %copy-done.13, f32[768]{0:T(1024)S(1)} %convert_element_type.389, ...), kind=kOutput, calls=%fused_computation.30 | convolution fusion | flops 2521694208 | bytes 22042624 | tf_op jit(solution)/shard_map/dot_general | solution.py:165
  217.3 44.8 %all-gather.45.cloned.1.call-done = bf16[1,3072,768]{2,1,0:T(8,128)(2,1)} async-done(((bf16[1,96,768]{2,1,0:T(8,128)(2,1)}), bf16[1,3072,768]{2,1,0:T(8,128)(2,1)}) %all-gather.45.cloned.1.call-update) | async-done | bytes 4718608 | tf_op jit(solution)/shard_map/all_gather | solution.py:260
  262.2 9.7 convert_reduce_fusion
  283.4 12.1 multiply_reduce_fusion
  295.6 7.2 multiply_convert_fusion
  315.1 8.7 all-gather.31.cloned.1.call-done
  348.0 31.4 %all-gather.33.cloned.1.call-done = bf16[1,768,768]{2,1,0:T(8,128)(2,1)} async-done(((bf16[1,24,768]{2,1,0:T(8,128)(2,1)}), bf16[1,768,768]{2,1,0:T(8,128)(2,1)}) %all-gather.33.cloned.1.call-update) | async-done | bytes 1179664 | tf_op jit(solution)/shard_map/all_gather | solution.py:254
  385.8 59.7 %all-gather.35.cloned.1.call-done = bf16[1,768,3072]{2,1,0:T(8,128)(2,1)} async-done(((bf16[1,24,3072]{2,1,0:T(8,128)(2,1)}), bf16[1,768,3072]{2,1,0:T(8,128)(2,1)}) %all-gather.35.cloned.1.call-update) | async-done | bytes 4718608 | tf_op jit(solution)/shard_map/all_gather | solution.py:258
  445.5 21.3 %multiply_convert_fusion.3 = (bf16[512,3072]{1,0:T(8,128)(2,1)}, f32[512,3072]{1,0:T(8,128)}, f32[512,3072]{1,0:T(8,128)}) fusion(f32[3072]{0:T(1024)S(1)} %copy-done.45, bf16[1,768,3072]{2,1,0:T(8,128)(2,1)} %all-gather.35.cloned.1.call-done, f32[512,768]{1,0:T(8,128)} %copy-done.15, f32[768]{0:T(1024)S(1)} %copy-done.54, f32[768]{0:T(1024)S(1)} %copy-done.41, ...), kind=kOutput, calls=%fused_computation.43 | convolution fusion | flops 2521694208 | bytes 22042624 | tf_op jit(solution)/shard_map/dot_general | solution.py:165
  466.8 44.7 %all-gather.37.cloned.1.call-done = bf16[1,3072,768]{2,1,0:T(8,128)(2,1)} async-done(((bf16[1,96,768]{2,1,0:T(8,128)(2,1)}), bf16[1,3072,768]{2,1,0:T(8,128)(2,1)}) %all-gather.37.cloned.1.call-update) | async-done | bytes 4718608 | tf_op jit(solution)/shard_map/all_gather | solution.py:260
  511.5 8.7 convert_reduce_fusion.1
  528.2 6.9 fusion.115
  540.9 12.4 multiply_reduce_fusion.1
  553.3 7.0 multiply_convert_fusion.1
  574.0 9.0 fusion.158
  583.0 9.0 fusion.157
  592.1 8.5 fusion.152
  601.0 8.5 fusion.149
  610.3 6.3 fusion.159
  619.4 41.7 %all-reduce.28 = (f32[768]{0:T(1024)S(1)}, f32[768]{0:T(1024)S(1)}, f32[768]{0:T(1024)S(1)}, f32[768]{0:T(1024)S(1)}, f32[768]{0:T(1024)S(1)}, /*index=5*/f32[76...) all-reduce(f32[768]{0:T(1024)S(1)} %get-tuple-element.169, ...), channel_id=25, replica_groups=mesh['fsdp'=32] {'fsdp'}, use_global_device_ids=true, to_apply=%region_30.31.clone | all-reduce | flops 15360 | bytes 122880
  665.6 6.8 fusion.105
  683.3 35.4 %reduce-scatter.13.cloned.1.call-done = f32[24,768]{1,0:T(8,128)} async-done(((f32[768,768]{1,0:T(8,128)}), f32[24,768]{1,0:T(8,128)}) %reduce-scatter.13.cloned.1.call-update) | async-done | bytes 73744 | tf_op jit(solution)/shard_map/reduce_scatter | solution.py:290
  720.3 122.2 %reduce-scatter.11.cloned.1.call-done = f32[24,2304]{1,0:T(8,128)} async-done(((f32[768,2304]{1,0:T(8,128)}), f32[24,2304]{1,0:T(8,128)}) %reduce-scatter.11.cloned.1.call-update) | async-done | bytes 221200 | tf_op jit(solution)/shard_map/reduce_scatter | solution.py:289
  842.5 124.8 %reduce-scatter.9.cloned.1.call-done = f32[24,2304]{1,0:T(8,128)} async-done(((f32[768,2304]{1,0:T(8,128)}), f32[24,2304]{1,0:T(8,128)}) %reduce-scatter.9.cloned.1.call-update) | async-done | bytes 221200 | tf_op jit(solution)/shard_map/reduce_scatter | solution.py:289
  969.2 138.9 %reduce-scatter.19.cloned.1.call-done = f32[24,3072]{1,0:T(8,128)} async-done(((f32[768,3072]{1,0:T(8,128)}), f32[24,3072]{1,0:T(8,128)}) %reduce-scatter.19.cloned.1.call-update) | async-done | bytes 294928 | tf_op jit(solution)/shard_map/reduce_scatter | solution.py:294
  1108.1 141.3 %reduce-scatter.17.cloned.1.call-done = f32[24,3072]{1,0:T(8,128)} async-done(((f32[768,3072]{1,0:T(8,128)}), f32[24,3072]{1,0:T(8,128)}) %reduce-scatter.17.cloned.1.call-update) | async-done | bytes 294928 | tf_op jit(solution)/shard_map/reduce_scatter | solution.py:294
  1251.3 138.5 %reduce-scatter.23.cloned.1.call-done = f32[96,768]{1,0:T(8,128)} async-done(((f32[3072,768]{1,0:T(8,128)}), f32[96,768]{1,0:T(8,128)}) %reduce-scatter.23.cloned.1.call-update) | async-done | bytes 294928 | tf_op jit(solution)/shard_map/reduce_scatter | solution.py:296
  1389.8 141.2 %reduce-scatter.21.cloned.1.call-done = f32[96,768]{1,0:T(8,128)} async-done(((f32[3072,768]{1,0:T(8,128)}), f32[96,768]{1,0:T(8,128)}) %reduce-scatter.21.cloned.1.call-update) | async-done | bytes 294928 | tf_op jit(solution)/shard_map/reduce_scatter | solution.py:296
  (328 shorter events, 151.6 us)
Async XLA Ops:
  7.2 15.7 %copy-start.2 = (bf16[2,512,768]{2,1,0:T(8,128)(2,1)S(1)}, bf16[2,512,768]{2,1,0:T(8,128)(2,1)}, u32[]{:S(2)}) copy-start(bf16[2,512,768]{2,1,0:T(8,128)(2,1)} %param.14) | copy-start | bytes 4718596
  7.2 67.5 %all-gather.39.cloned.1.call-start = ((), (), s32[]{:S(2)}) async-start(), calls=%async_computation.20 | async-start | bytes 3649536 | tf_op jit(solution)/shard_map/all_gather | solution.py:253
  9.0 121.2 %all-gather.41.cloned.1.call-start = ((), (), s32[]{:S(2)}) async-start(), calls=%async_computation.21 | async-start | bytes 1216512 | tf_op jit(solution)/shard_map/all_gather | solution.py:254
  10.5 185.8 %all-gather.43.cloned.1.call-start = ((), (), s32[]{:S(2)}) async-start(), calls=%async_computation.22 | async-start | bytes 4866048 | tf_op jit(solution)/shard_map/all_gather | solution.py:258
  12.3 249.9 %all-gather.45.cloned.1.call-start = ((), (), s32[]{:S(2)}) async-start(), calls=%async_computation.23 | async-start | bytes 4866048 | tf_op jit(solution)/shard_map/all_gather | solution.py:260
  14.1 309.7 %all-gather.31.cloned.1.call-start = ((), (), s32[]{:S(2)}) async-start(), calls=%async_computation.16 | async-start | bytes 3649536 | tf_op jit(solution)/shard_map/all_gather | solution.py:253
  14.7 364.8 %all-gather.33.cloned.1.call-start = ((), (), s32[]{:S(2)}) async-start(), calls=%async_computation.17 | async-start | bytes 1216512 | tf_op jit(solution)/shard_map/all_gather | solution.py:254
  15.3 430.3 %all-gather.35.cloned.1.call-start = ((), (), s32[]{:S(2)}) async-start(), calls=%async_computation.18 | async-start | bytes 4866048 | tf_op jit(solution)/shard_map/all_gather | solution.py:258
  16.0 495.5 %all-gather.37.cloned.1.call-start = ((), (), s32[]{:S(2)}) async-start(), calls=%async_computation.19 | async-start | bytes 4866048 | tf_op jit(solution)/shard_map/all_gather | solution.py:260
  16.8 666.5 %reduce-scatter.15.cloned.1.call-start = ((), (), s32[]{:S(2)}) async-start(), calls=%async_computation.11 | async-start | bytes 2433024 | tf_op jit(solution)/shard_map/reduce_scatter | solution.py:290
  24.1 56.6 %copy-start.50 = (f32[512]{0:T(512)}, f32[512]{0:T(512)S(1)}, u32[]{:S(2)}) copy-start(f32[512]{0:T(512)S(1)} %fusion.147) | copy-start | bytes 6148
  71.3 204.1 %copy-start.42 = (f32[768]{0:T(1024)}, f32[768]{0:T(1024)S(1)}, u32[]{:S(2)}) copy-start(f32[768]{0:T(1024)S(1)} %convert_element_type.388) | copy-start | bytes 9220
  71.9 124.4 %copy-start.55 = (f32[768]{0:T(1024)}, f32[768]{0:T(1024)S(1)}, u32[]{:S(2)}) copy-start(f32[768]{0:T(1024)S(1)} %convert_element_type.389) | copy-start | bytes 9220
  98.1 34.7 %copy-start.29 = (bf16[12,64,512]{2,1,0:T(8,128)(2,1)}, bf16[12,64,512]{2,1,0:T(8,128)(2,1)S(1)}, u32[]{:S(2)}) copy-start(bf16[12,64,512]{2,1,0:T(8,128)(2,1)S(1)} %fusion.100) | copy-start | bytes 2359300
  132.5 143.0 %copy-start.32 = (f32[512]{0:T(512)}, f32[512]{0:T(512)S(1)}, u32[]{:S(2)}) copy-start(f32[512]{0:T(512)S(1)} %broadcast_multiply_fusion) | copy-start | bytes 6148
  133.6 141.8 %copy-start.46 = (f32[512]{0:T(512)}, f32[512]{0:T(512)S(1)}, u32[]{:S(2)}) copy-start(f32[512]{0:T(512)S(1)} %fusion.148) | copy-start | bytes 6148
  133.6 128.6 %copy-start.7 = (bf16[2,512,768]{2,1,0:T(8,128)(2,1)S(1)}, bf16[2,512,768]{2,1,0:T(8,128)(2,1)}, u32[]{:S(2)}) copy-start(bf16[2,512,768]{2,1,0:T(8,128)(2,1)} %param.16) | copy-start | bytes 4718596
  315.1 14.3 copy-start.48
  343.7 35.8 %copy-start.59 = (f32[768]{0:T(1024)S(1)}, f32[768]{0:T(1024)}, u32[]{:S(2)}) copy-start(f32[768]{0:T(1024)} %convert_element_type.380) | copy-start | bytes 9220
  383.5 62.0 %copy-start.41 = (f32[768]{0:T(1024)S(1)}, f32[768]{0:T(1024)}, u32[]{:S(2)}) copy-start(f32[768]{0:T(1024)} %convert_element_type.381) | copy-start | bytes 9220
  383.5 62.0 %copy-start.45 = (f32[3072]{0:T(1024)S(1)}, f32[3072]{0:T(1024)}, u32[]{:S(2)}) copy-start(f32[3072]{0:T(1024)} %convert_element_type.383) | copy-start | bytes 36868
  383.5 62.0 %copy-start.54 = (f32[768]{0:T(1024)S(1)}, f32[768]{0:T(1024)}, u32[]{:S(2)}) copy-start(f32[768]{0:T(1024)} %convert_element_type.382) | copy-start | bytes 9220
  385.7 333.0 %reduce-scatter.13.cloned.1.call-start = ((), (), s32[]{:S(2)}) async-start(), calls=%async_computation.10 | async-start | bytes 2433024 | tf_op jit(solution)/shard_map/reduce_scatter | solution.py:290
  528.1 314.4 %reduce-scatter.11.cloned.1.call-start = ((), (), s32[]{:S(2)}) async-start(), calls=%async_computation.9 | async-start | bytes 7299072 | tf_op jit(solution)/shard_map/reduce_scatter | solution.py:289
  535.1 432.3 %reduce-scatter.9.cloned.1.call-start = ((), (), s32[]{:S(2)}) async-start(), calls=%async_computation.8 | async-start | bytes 7299072 | tf_op jit(solution)/shard_map/reduce_scatter | solution.py:289
  540.9 12.4 slice-start
  540.9 12.4 slice-start.1
  540.9 12.4 slice-start.2
  573.3 534.8 %reduce-scatter.19.cloned.1.call-start = ((), (), s32[]{:S(2)}) async-start(), calls=%async_computation.13 | async-start | bytes 9732096 | tf_op jit(solution)/shard_map/reduce_scatter | solution.py:294
  583.0 666.4 %reduce-scatter.17.cloned.1.call-start = ((), (), s32[]{:S(2)}) async-start(), calls=%async_computation.12 | async-start | bytes 9732096 | tf_op jit(solution)/shard_map/reduce_scatter | solution.py:294
  592.1 797.7 %reduce-scatter.23.cloned.1.call-start = ((), (), s32[]{:S(2)}) async-start(), calls=%async_computation.15 | async-start | bytes 9732096 | tf_op jit(solution)/shard_map/reduce_scatter | solution.py:296
  600.7 930.4 %reduce-scatter.21.cloned.1.call-start = ((), (), s32[]{:S(2)}) async-start(), calls=%async_computation.14 | async-start | bytes 9732096 | tf_op jit(solution)/shard_map/reduce_scatter | solution.py:296
  (60 other events, 245.8 us)
Sparse Core Ops, SparseCore 0:
  11.5 62.9 all-gather.38
  77.4 52.8 all-gather.40
  133.7 62.5 all-gather.42
  199.7 62.4 all-gather.44
  264.9 58.8 all-gather.30
  326.6 52.8 all-gather.32
  382.9 62.5 all-gather.34
  449.0 62.4 all-gather.36
  516.8 97.8 reduce-scatter.14
  620.7 97.9 reduce-scatter.12
  724.4 118.0 reduce-scatter.10
  849.0 118.3 reduce-scatter.8
  973.3 134.7 reduce-scatter.18
  1114.8 134.5 reduce-scatter.16
  1255.1 134.6 reduce-scatter.22
  1396.6 134.4 reduce-scatter.20
where the time goes:
time: 1550 us; the launch traced here: 1540 us
  waiting for transfers between devices  1130 us (73%)
  matrix products  216 us (14%)
  blocking collectives  85.9 us (6%)
  local copies, waits for them, and re-layouts  47.2 us (3%)
  other arithmetic  44.7 us (3%)
    reduce_scatter x2, waiting for transfers between devices, local(): lax.psum_scatter(weight_grads[7], 'fsdp', scatter_dimension=0, tiled=True)  280 us
    reduce_scatter x2, waiting for transfers between devices, local(): lax.psum_scatter(weight_grads[9], 'fsdp', scatter_dimension=0, tiled=True)  280 us
    reduce_scatter x2, waiting for transfers between devices, local(): lax.psum_scatter(weight_grads[2], 'fsdp', scatter_dimension=0, tiled=True)  247 us
    all_gather x2, waiting for transfers between devices, local(): lax.all_gather(w_fc1[modality], 'fsdp', axis=0, tiled=True)  122 us
    all_gather x2, waiting for transfers between devices, local(): lax.all_gather(w_fc2[modality], 'fsdp', axis=0, tiled=True)  89.5 us
    unnamed x2, blocking collectives  85.9 us
    all_gather x2, waiting for transfers between devices, local(): lax.all_gather(w_proj[modality], 'fsdp', axis=0, tiled=True)  63.5 us
    dot_general x8, matrix products, contract_rows(): lax.dot_general(left, right, (((0,), (0,)), ((), ())), preferred_element_...  51.5 us
  transfers between devices with their start and end apart: 16, of which 14 were waited for; matrix products, arithmetic and copies ran while one was open for 19% of the time, Pallas kernels for 0%

commit v1 on v0

v1 whole, which is shorter than its diff:
```python
import functools

import jax
import jax.numpy as jnp
from jax import lax
from jax.experimental import pallas as pl
from jax.experimental.pallas import tpu as pltpu
from jax.sharding import PartitionSpec as P

HEADS = 12
SIDE_S = 12
SIDE_M = 15
SIDE_L = 20
RING = 32
MESH = pl.DeviceIdType.MESH
BF = jnp.bfloat16
F32 = jnp.float32
FAR = 1e33


def packing(kind_ids, row_count):
    slot_count = kind_ids.shape[0]
    sides = jnp.where(kind_ids == 0, SIDE_S, jnp.where(kind_ids == 1, SIDE_M, SIDE_L)).astype(
        jnp.int32
    )
    lengths = sides * sides
    slots = jnp.arange(slot_count, dtype=jnp.int32)
    ends = jnp.sum(jnp.where(slots[None, :] <= slots[:, None], lengths[None, :], 0), axis=1)
    starts = ends - lengths
    places = jnp.arange(row_count, dtype=jnp.int32)
    inside = (
        (ends <= row_count)[None, :]
        & (places[:, None] >= starts[None, :])
        & (places[:, None] < ends[None, :])
    ).astype(jnp.int32)
    filled = jnp.sum(inside, axis=1)
    segment = jnp.sum(inside * slots[None, :], axis=1) + (1 - filled) * (slot_count + places)
    offset = places - jnp.sum(inside * starts[None, :], axis=1)
    side = jnp.sum(inside * sides[None, :], axis=1) + (1 - filled)
    return segment, offset // side, offset % side, filled


class Place:
    def __init__(self, spread):
        me = lax.axis_index("fsdp")
        rest = lax.rem(me, spread)
        p = me // spread
        self.p = p
        self.c = lax.rem(p, 2)
        self.x = lax.rem(p // 2, 2)
        self.y = lax.rem(p // 4, 2)
        self.m = lax.rem(p // 8, 2)
        self.z = lax.rem(p // 16, 2)
        dev = lambda q: (q * spread + rest,)
        sib = p + 1 - 2 * self.c
        pair = p + 8 * (1 - 2 * self.m)
        self.sib = dev(sib)
        self.xn = dev(p + 2 * (1 - 2 * self.x))
        self.yn = dev(p + 4 * (1 - 2 * self.y))
        self.zn = dev(p + 16 * (1 - 2 * self.z))
        self.pair = dev(pair)
        self.cross = dev(pair + 1 - 2 * self.c)

    def chip(self, fz, fc, fy, fx):
        flip = lambda v, f: 1 - v if f else v
        return (
            (flip(self.z, fz) * 2 + flip(self.c, fc)) * 2 + flip(self.y, fy)
        ) * 2 + flip(self.x, fx)

    def greet(self):
        barrier = pltpu.get_barrier_semaphore()
        everyone = (self.sib, self.xn, self.yn, self.zn, self.pair, self.cross)
        for other in everyone:
            pl.semaphore_signal(barrier, inc=1, device_id=other, device_id_type=MESH)
        pl.semaphore_wait(barrier, len(everyone))


OWN, ZB, X0, X1, Y0, Y1, D0, D1 = range(8)
FLIPS = ((0, 0, 0), (1, 0, 0), (0, 0, 1), (1, 0, 1), (0, 1, 0), (1, 1, 0), (0, 1, 1), (1, 1, 1))


def rcopy(src, dst, ssem, rsem, dev):
    return pltpu.make_async_remote_copy(
        src_ref=src, dst_ref=dst, send_sem=ssem, recv_sem=rsem, device_id=dev, device_id_type=MESH
    )


class Gather:
    def __init__(self, place, full, rows, ssem, rsem):
        self.pl, self.full, self.rows, self.ssem, self.rsem = place, full, rows, ssem, rsem

    def block(self, kind, other=0):
        fz, fy, fx = FLIPS[kind]
        start = self.pl.chip(fz, other, fy, fx) * self.rows
        return self.full.at[pl.ds(pl.multiple_of(start, self.rows), self.rows)]

    def send(self, kind, way):
        place = self.pl
        if way == "s":
            dev, slot = place.sib, 8 + kind
        else:
            dev = {"x": place.xn, "y": place.yn, "z": place.zn}[way]
            fz, fy, fx = FLIPS[kind]
            flips = {"x": (fz, fy, 1 - fx), "y": (fz, 1 - fy, fx), "z": (1 - fz, fy, fx)}[way]
            slot = FLIPS.index(flips)
        view = self.block(kind)
        return rcopy(view, view, self.ssem.at[slot], self.rsem.at[slot], dev)

    AFTER = {
        OWN: "zxys",
        ZB: "xys",
        X0: "ys",
        X1: "s",
        Y0: "s",
        Y1: "xs",
        D0: "s",
        D1: "s",
    }

    def start(self, kind):
        for way in self.AFTER[kind]:
            self.send(kind, way).start()

    def arrived(self, kind, other=0):
        view = self.block(kind, other)
        slot = kind + 8 * other
        rcopy(view, view, self.ssem.at[slot], self.rsem.at[slot], self.pl.sib).wait_recv()

    def finish(self):
        for kind in range(8):
            for way in self.AFTER[kind]:
                self.send(kind, way).wait_send()


def hand_in(place, shard, spot, c_rows, ssem, rsem, go):
    mine, theirs = shard.at[place.m], shard.at[1 - place.m]
    here = lambda: pltpu.make_async_copy(mine, spot(place.c), rsem.at[place.c])
    to_sib = lambda: rcopy(mine, spot(place.c), ssem.at[0], rsem.at[place.c], place.sib)
    to_pair = lambda: rcopy(theirs, spot(place.c), ssem.at[1], rsem.at[place.c], place.pair)
    to_cross = lambda: rcopy(theirs, spot(place.c), ssem.at[1], rsem.at[place.c], place.cross)
    if go == "start":

        @pl.when(place.c == place.m)
        def _():
            here().start()
            to_pair().start()

        @pl.when(place.c != place.m)
        def _():
            to_sib().start()
            to_cross().start()

    elif go == "recv":
        for piece in range(2):
            dst = spot(piece)
            rcopy(dst, dst, ssem.at[1], rsem.at[piece], place.sib).wait_recv()
    else:

        @pl.when(place.c != place.m)
        def _():
            to_sib().wait_send()

        to_pair().wait_send()


def ag_kernel(spread, *refs):
    (pat, dog, lay, wq, wp, w1, w2, sm, pat_o, dog_o, lay_o, fq, fp, f1, f2, fs) = refs[:16]
    (gq, gp, g1, hs, hr, ss, rs, as_, ar) = refs[16:]
    place = Place(spread)
    place.greet()
    hand = (
        (sm, fs, None, 16),
        (wq, fq, gq, 24),
        (wp, fp, gp, 24),
        (w1, f1, g1, 24),
        (w2, f2, None, w2.shape[1]),
    )
    gathers = [
        Gather(place, full, 2 * rows, ss.at[k], rs.at[k])
        for k, (_, full, _, rows) in enumerate(hand)
    ]

    def spot_of(k):
        _, full, stage, rows = hand[k]
        if stage is not None:
            return lambda piece: stage.at[piece]
        own = place.chip(0, 0, 0, 0) * 2

        def spot(piece):
            place_of = place.p if piece is place.c else own + piece
            return full.at[pl.ds(pl.multiple_of(place_of * rows, 16), rows)]

        return spot

    acts = [
        rcopy(pat.at[1 - place.m], pat_o, as_.at[0], ar.at[0], place.pair),
        rcopy(lay, lay_o, as_.at[2], ar.at[2], place.pair),
        rcopy(dog.at[1 - place.m], dog_o, as_.at[1], ar.at[1], place.pair),
    ]
    for k in range(5):
        hand_in(place, hand[k][0], spot_of(k), hand[k][3], hs.at[k], hr.at[k], "start")
    for act in acts:
        act.start()
    for k in range(5):
        hand_in(place, hand[k][0], spot_of(k), hand[k][3], hs.at[k], hr.at[k], "recv")
        _, full, stage, rows = hand[k]
        if stage is not None:
            both = jnp.concatenate([stage[0].astype(F32), stage[1].astype(F32)], axis=0)
            start = pl.multiple_of(place.chip(0, 0, 0, 0) * (2 * rows), 2 * rows)
            full[pl.ds(start, 2 * rows), :] = both.astype(BF)
        gathers[k].start(OWN)
    for k in range(5):
        for kind in (ZB, X0, Y0, X1, Y1, D0, D1):
            gathers[k].arrived(kind)
            gathers[k].start(kind)
    for k in range(5):
        for kind in range(8):
            gathers[k].arrived(kind, 1)
    for k in range(5):
        hand_in(place, hand[k][0], spot_of(k), hand[k][3], hs.at[k], hr.at[k], "send")
        gathers[k].finish()
    for act in acts:
        act.wait()


def all_gather(spread, pat, dog, lay, wq, wp, w1, w2, sm):
    any_, vm = pl.BlockSpec(memory_space=pl.ANY), pl.BlockSpec(memory_space=pltpu.VMEM)
    d = pat.shape[2]
    f32, bf = jnp.float32, BF
    out = [
        jax.ShapeDtypeStruct(pat.shape[1:], bf),
        jax.ShapeDtypeStruct(pat.shape[1:], bf),
        jax.ShapeDtypeStruct(lay.shape, f32),
        jax.ShapeDtypeStruct((d, wq.shape[2]), bf),
        jax.ShapeDtypeStruct((d, wp.shape[2]), bf),
        jax.ShapeDtypeStruct((d, w1.shape[2]), bf),
        jax.ShapeDtypeStruct((w2.shape[1] * RING, d), bf),
        jax.ShapeDtypeStruct((RING * 16, 128), bf),
    ]
    dma = pltpu.SemaphoreType.DMA
    return pl.pallas_call(
        functools.partial(ag_kernel, spread),
        out_shape=out,
        in_specs=[any_] * 8,
        out_specs=[any_, any_, any_] + [vm] * 5,
        scratch_shapes=[
            pltpu.VMEM((2, 24, wq.shape[2]), bf),
            pltpu.VMEM((2, 24, wp.shape[2]), bf),
            pltpu.VMEM((2, 24, w1.shape[2]), bf),
            dma((5, 2)),
            dma((5, 2)),
            dma((5, 16)),
            dma((5, 16)),
            dma((3,)),
            dma((3,)),
        ],
        compiler_params=pltpu.CompilerParams(
            collective_id=0, has_side_effects=True, vmem_limit_bytes=48 * 2**20
        ),
        name="gather",
    )(pat, dog, lay, wq, wp, w1, w2, sm)


class Scatter:
    def __init__(self, place, full, rows, got_sib, got, ssem, rsem):
        self.pl, self.full, self.rows = place, full, rows
        self.got_sib, self.got, self.ssem, self.rsem = got_sib, got, ssem, rsem

    def start_of(self, kind):
        fz, fy, fx = FLIPS[kind]
        return pl.multiple_of(self.pl.chip(fz, 0, fy, fx) * self.rows, self.rows)

    def plane(self, z, other):
        c = 1 - self.pl.c if other else self.pl.c
        return pl.ds(pl.multiple_of((z * 2 + c) * (4 * self.rows), self.rows), 4 * self.rows)

    def sib(self, z):
        return rcopy(
            self.full.at[self.plane(z, 1)],
            self.got_sib.at[z],
            self.ssem.at[z],
            self.rsem.at[z],
            self.pl.sib,
        )

    MOVES = {D0: ("y", 0), D1: ("x", 1), X0: ("x", 2), X1: ("x", 3), Y0: ("y", 4), Y1: ("y", 5), ZB: ("z", 6)}

    def move(self, kind):
        way, slot = self.MOVES[kind]
        dev = {"x": self.pl.xn, "y": self.pl.yn, "z": self.pl.zn}[way]
        return rcopy(
            self.full.at[pl.ds(self.start_of(kind), self.rows)],
            self.got.at[slot],
            self.ssem.at[2 + slot],
            self.rsem.at[2 + slot],
            dev,
        )

    def add(self, kind, slots):
        rows = pl.ds(self.start_of(kind), self.rows)
        total = self.full[rows, :].astype(F32)
        for slot in slots:
            total = total + self.got[slot].astype(F32)
        self.full[rows, :] = total.astype(BF)

    def begin(self):
        self.sib(0).start()
        self.sib(1).start()

    def second(self):
        for z in range(2):
            self.sib(z).wait()
        step = 16

        for z in range(2):
            base = (z * 2 + self.pl.c) * (4 * self.rows)

            @pl.loop(0, 4 * self.rows // step)
            def _(i, z=z, base=base):
                rows = pl.ds(pl.multiple_of(base + i * step, step), step)
                theirs = self.got_sib[z, pl.ds(pl.multiple_of(i * step, step), step), :]
                self.full[rows, :] = (self.full[rows, :].astype(F32) + theirs.astype(F32)).astype(BF)

        for kind in (D0, D1, X1, Y0):
            self.move(kind).start()

    def third(self):
        self.move(D0).wait()
        self.add(X0, (0,))
        self.move(X0).start()
        self.move(D1).wait()
        self.add(Y1, (1,))
        self.move(Y1).start()

    def fourth(self):
        self.move(X1).wait()
        self.move(Y1).wait()
        self.add(ZB, (3, 5))
        self.move(ZB).start()

    def total(self):
        self.move(X0).wait()
        self.move(Y0).wait()
        self.move(ZB).wait()
        rows = pl.ds(self.start_of(OWN), self.rows)
        total = self.full[rows, :].astype(F32)
        for slot in (2, 4, 6):
            total = total + self.got[slot].astype(F32)
        return total


def hand_back(place, stage, out, ssem, rsem, go):
    if go == "start":

        @pl.when(place.c == place.m)
        def _():
            pltpu.make_async_copy(stage.at[place.c], out.at[place.m], rsem.at[place.m]).start()
            rcopy(
                stage.at[1 - place.c], out.at[place.m], ssem.at[0], rsem.at[place.m], place.sib
            ).start()

        @pl.when(place.c != place.m)
        def _():
            rcopy(
                stage.at[place.c], out.at[place.m], ssem.at[0], rsem.at[place.m], place.pair
            ).start()
            rcopy(
                stage.at[1 - place.c], out.at[place.m], ssem.at[1], rsem.at[place.m], place.cross
            ).start()

    elif go == "recv":
        for k in range(2):
            rcopy(out.at[k], out.at[k], ssem.at[0], rsem.at[k], place.sib).wait_recv()
    else:
        rcopy(stage.at[0], out.at[0], ssem.at[0], rsem.at[0], place.sib).wait_send()

        @pl.when(place.c != place.m)
        def _():
            rcopy(stage.at[0], out.at[0], ssem.at[1], rsem.at[0], place.sib).wait_send()


def rs_kernel(spread, *refs):
    (gq, gp, g1, g2, gs, enc, pgr) = refs[:7]
    (oq, op, o1, o2, os_, enc_o, pgr_o) = refs[7:14]
    scratch = refs[14:]
    got_sib, got, stages = scratch[0:4], scratch[4:8], scratch[8:12]
    (sgot, ss, rs, hs, hr, es, er, ts, tr) = scratch[12:]
    place = Place(spread)
    place.greet()
    acts = [
        rcopy(enc, enc_o, es.at[0], er.at[0], place.pair),
        rcopy(pgr, pgr_o, es.at[1], er.at[1], place.pair),
    ]
    for act in acts:
        act.start()
    order = (3, 2, 1, 0)
    fulls = (gq, gp, g1, g2)
    outs = (oq, op, o1, o2)
    rows = (48, 48, 48, g2.shape[0] // 16)
    sc = [
        Scatter(place, fulls[k], rows[k], got_sib[k], got[k], ss.at[k], rs.at[k]) for k in range(4)
    ]
    for k in order:
        sc[k].begin()
    os_[place.m] = gs[...]
    for i, dev in enumerate((place.sib, place.xn, place.yn, place.zn)):
        copy = rcopy(os_.at[place.m], sgot.at[i], ts.at[i], tr.at[i], dev)
        copy.start()
        copy.wait()
        os_[place.m] = os_[place.m] + sgot[i]
    copy = rcopy(os_.at[place.m], os_.at[place.m], ts.at[4], tr.at[4], place.pair)
    copy.start()
    for k in order:
        sc[k].second()
    for k in order:
        sc[k].third()
    for k in order:
        sc[k].fourth()
    for k in order:
        total = sc[k].total()
        half = rows[k] // 2
        stages[k][0] = total[:half].astype(BF)
        stages[k][1] = total[half:].astype(BF)
        hand_back(place, stages[k], outs[k], hs.at[k], hr.at[k], "start")
    for k in order:
        hand_back(place, stages[k], outs[k], hs.at[k], hr.at[k], "recv")
        hand_back(place, stages[k], outs[k], hs.at[k], hr.at[k], "send")
    copy.wait_send()
    theirs = os_.at[1 - place.m]
    rcopy(theirs, theirs, ts.at[4], tr.at[4], place.pair).wait_recv()
    for act in acts:
        act.wait()


def reduce_scatter(spread, gq, gp, g1, g2, gs, enc, pgr):
    any_, vm = pl.BlockSpec(memory_space=pl.ANY), pl.BlockSpec(memory_space=pltpu.VMEM)
    d = gq.shape[0]
    fulls = (gq, gp, g1, g2)
    rows = [g.shape[0] // 16 for g in fulls]
    out = [jax.ShapeDtypeStruct((2, r // 2, g.shape[1]), BF) for r, g in zip(rows, fulls)]
    out += [
        jax.ShapeDtypeStruct((2,) + gs.shape, F32),
        jax.ShapeDtypeStruct(enc.shape, BF),
        jax.ShapeDtypeStruct(pgr.shape, BF),
    ]
    dma = pltpu.SemaphoreType.DMA
    return pl.pallas_call(
        functools.partial(rs_kernel, spread),
        out_shape=out,
        in_specs=[vm] * 5 + [any_] * 2,
        out_specs=[any_] * 4 + [vm] + [any_] * 2,
        scratch_shapes=[pltpu.VMEM((2, 4 * r, g.shape[1]), BF) for r, g in zip(rows, fulls)]
        + [pltpu.VMEM((7, r, g.shape[1]), BF) for r, g in zip(rows, fulls)]
        + [pltpu.VMEM((2, r // 2, g.shape[1]), BF) for r, g in zip(rows, fulls)]
        + [
            pltpu.VMEM((4,) + gs.shape, F32),
            dma((4, 9)),
            dma((4, 9)),
            dma((4, 2)),
            dma((4, 2)),
            dma((2,)),
            dma((2,)),
            dma((5,)),
            dma((5,)),
        ],
        compiler_params=pltpu.CompilerParams(
            collective_id=1, has_side_effects=True, vmem_limit_bytes=56 * 2**20
        ),
        name="scatter",
    )(gq, gp, g1, g2, gs, enc, pgr)


def small_pack(parts, b1):
    rows = jnp.stack([jnp.pad(v, ((0, 0), (0, 128 - v.shape[1]))) for v in (*parts, b1)], axis=1)
    return jnp.pad(rows, ((0, 0), (0, 16 - rows.shape[1]), (0, 0)))


def norm_stats(v):
    mean = jnp.mean(v, axis=-1, keepdims=True)
    center = v - mean
    r = lax.rsqrt(jnp.mean(center * center, axis=-1, keepdims=True) + 1e-06)
    return center * r, r


def norm_back(dn, nhat, r, gain):
    dh = dn * gain
    row = r * (
        dh - jnp.mean(dh, axis=-1, keepdims=True) - nhat * jnp.mean(dh * nhat, axis=-1, keepdims=True)
    )
    return row, jnp.sum(dn * nhat, axis=0), jnp.sum(dn, axis=0)


def mm(a, b, ca, cb):
    return lax.dot_general(a, b, (((ca,), (cb,)), ((), ())), preferred_element_type=F32)


def compute(xs, dos, lays, wq, wp, w1, w2, vecs, b1):
    d = xs.shape[1]
    rows = lays.shape[2]
    hd = d // HEADS
    g1n, b1n, bp, g2n, b2n, bf2 = (vecs[i] for i in range(6))
    seg, gr, gc, live = (lays[:, i] for i in range(4))
    dist = jnp.sqrt(
        (gr[:, :, None] - gr[:, None, :]) ** 2 + (gc[:, :, None] - gc[:, None, :]) ** 2
    )
    dist = jnp.where(seg[:, :, None] == seg[:, None, :], dist, FAR)
    slopes = jnp.exp2(-8.0 * (jnp.arange(HEADS, dtype=F32) + 1.0) / HEADS)
    x = xs.astype(F32)
    n1, r1 = norm_stats(x)
    a = (n1 * g1n + b1n).astype(BF)
    qkv = mm(a, wq, 1, 0).astype(BF)
    heads = qkv.reshape(2, rows, 3, HEADS, hd)
    q, k, v = heads[:, :, 0], heads[:, :, 1], heads[:, :, 2]
    s = (
        jnp.einsum("gqhd,gkhd->ghqk", q, k, preferred_element_type=F32) * hd**-0.5
        - slopes[None, :, None, None] * dist[:, None]
    )
    prob = jax.nn.softmax(s, axis=-1)
    pb = prob.astype(BF)
    o = jnp.einsum("ghqk,gkhd->gqhd", pb, v, preferred_element_type=F32).astype(BF)
    o = o.reshape(2 * rows, d)
    y1 = x + (mm(o, wp, 1, 0) + bp)
    n2, r2 = norm_stats(y1)
    c = (n2 * g2n + b2n).astype(BF)
    u = mm(c, w1, 1, 0) + b1
    phi = 0.5 * (1.0 + lax.erf(u * 2**-0.5))
    g = (u * phi).astype(BF)
    slope = phi + u * (jnp.exp(-0.5 * u * u) * 0.3989422804014327)
    y = y1 + (mm(g, w2, 1, 0) + bf2)
    dy = dos.astype(F32) * live.reshape(-1, 1)
    dz = dy.astype(BF)
    gw2 = mm(g, dz, 0, 0).astype(BF)
    dg = mm(dz, w2, 1, 1)
    du = (dg * slope).astype(BF)
    gw1 = mm(c, du, 0, 0).astype(BF)
    dc = mm(du, w1, 1, 1)
    row, gg2, gb2 = norm_back(dc, n2, r2, g2n)
    dy1 = dy + row
    dy1r = dy1.astype(BF)
    gwp = mm(o, dy1r, 0, 0).astype(BF)
    do = mm(dy1r, wp, 1, 1).astype(BF).reshape(2, rows, HEADS, hd)
    dv = jnp.einsum("ghqk,gqhd->gkhd", pb, do, preferred_element_type=F32)
    dp = jnp.einsum("gqhd,gkhd->ghqk", do, v, preferred_element_type=F32)
    ds = (prob * (dp - jnp.sum(prob * dp, axis=-1, keepdims=True))).astype(BF)
    dq = jnp.einsum("ghqk,gkhd->gqhd", ds, k, preferred_element_type=F32) * hd**-0.5
    dk = jnp.einsum("ghqk,gqhd->gkhd", ds, q, preferred_element_type=F32) * hd**-0.5
    dqkv = jnp.stack([dq, dk, dv], axis=2).reshape(2 * rows, 3 * d).astype(BF)
    gwq = mm(a, dqkv, 0, 0).astype(BF)
    da = mm(dqkv, wq, 1, 1)
    row, gg1, gb1 = norm_back(da, n1, r1, g1n)
    sums = [
        gg1,
        gb1,
        jnp.sum(dy1r.astype(F32), axis=0),
        gg2,
        gb2,
        jnp.sum(dz.astype(F32), axis=0),
    ]
    bias1 = jnp.sum(du.astype(F32), axis=0).reshape(-1, d)
    small = jnp.concatenate([jnp.stack(sums), bias1], axis=0)
    small = jnp.pad(small, ((0, 16 - small.shape[0]), (0, 0)))
    return y.astype(BF), (dy1 + row).astype(BF), gwq, gwp, gw1, gw2, small


def local(
    count, patches, tile_kind, out_grad, n1g, n1b, wq, wp, bp, n2g, n2b, w1, b1, w2, b2
):
    spread = count // RING
    idx = lax.axis_index("fsdp")
    p = idx // spread
    m = (p // 8) % 2
    rows, d = patches.shape[1:]
    parts = (n1g, n1b, bp, n2g, n2b, b2)
    if spread > 1:
        groups = [[q * spread + j for j in range(spread)] for q in range(RING)]
        ag = functools.partial(
            lax.all_gather, axis_name="fsdp", axis=1, tiled=True, axis_index_groups=groups
        )
        wq, wp, w1, w2, b1 = ag(wq), ag(wp), ag(w1), ag(w2), ag(b1)
        parts = tuple(ag(v) for v in parts)
    lay = jnp.stack([v.astype(F32) for v in packing(tile_kind, rows)])
    lay = jnp.pad(lay, ((0, 4), (0, 0)))
    sm = small_pack(parts, b1)
    pat2, dog2, lay2, fq, fp, f1, f2, fs = all_gather(
        spread, patches, out_grad, lay, wq, wp, w1, w2, sm
    )
    own = b2.shape[1] * spread
    fs = fs.astype(F32).reshape(RING, 16, 128)
    vecs = fs[:, :6, : d // RING].transpose(1, 0, 2).reshape(6, d)
    hb = fs[:, 6, : w2.shape[1]].reshape(-1)
    mine = lambda v: lax.dynamic_index_in_dim(v, m, 0, keepdims=False)
    y, pg, gq, gp, g1, g2, gs = compute(
        jnp.concatenate([mine(patches), pat2]),
        jnp.concatenate([mine(out_grad), dog2]),
        jnp.stack([lay, lay2]),
        fq, fp, f1, f2, vecs, hb,
    )
    oq, op, o1, o2, os_, enc2, pg2 = reduce_scatter(
        spread, gq, gp, g1, g2, gs, y[rows:], pg[rows:]
    )
    order = lambda a, b: jnp.where(m == 0, jnp.stack([a, b]), jnp.stack([b, a]))
    encoded = order(y[:rows], enc2)
    pgrad = order(pg[:rows], pg2).astype(F32)
    seg = d // RING
    vec = lax.dynamic_slice_in_dim(os_[:, :6], p * seg, seg, axis=2)
    hid = os_[:, 6 : 6 + w2.shape[1] * RING // d].reshape(2, -1)
    hid = lax.dynamic_slice_in_dim(hid, p * w2.shape[1], w2.shape[1], axis=1)
    grads = [oq.astype(F32), op.astype(F32), o1.astype(F32), o2.astype(F32)]
    if spread > 1:
        rs = functools.partial(
            lax.psum_scatter, axis_name="fsdp", tiled=True, axis_index_groups=groups
        )
        grads = [rs(v, scatter_dimension=1) for v in grads]
        vec, hid = rs(vec, scatter_dimension=2), rs(hid, scatter_dimension=1)
    return (
        encoded,
        pgrad,
        vec[:, 0],
        vec[:, 1],
        grads[0],
        grads[1],
        vec[:, 2],
        vec[:, 3],
        vec[:, 4],
        grads[2],
        hid,
        grads[3],
        vec[:, 5],
    )


def solution(mesh):
    three, two = P(None, "fsdp", None), P(None, "fsdp")
    in_specs = (three, P("fsdp"), three, two, two, three, three, two, two, two, three, two, three, two)
    out_specs = (three, three, two, two, three, three, two, two, two, three, two, three, two)
    return jax.shard_map(
        functools.partial(local, mesh.shape["fsdp"]),
        mesh=mesh,
        in_specs=in_specs,
        out_specs=out_specs,
        check_vma=False,
    )
```

time: 1550 us -> 519 us (0.33)
  waiting for transfers between devices: 1130 us -> 0 us
  Pallas kernels: 0 us -> 252 us
  blocking collectives: 85.9 us -> 0 us
  matrix products: 216 us -> 160 us
    reduce_scatter x8 -> x0, waiting for transfers between devices: 842 us -> none  [the longest x2 280 us: local(): lax.psum_scatter(weight_grads[7], 'fsdp', scatter_dimension=0, tiled=True)]
    all_gather x8 -> x0, waiting for transfers between devices: 284 us -> none  [the longest x2 122 us: local(): lax.all_gather(w_fc1[modality], 'fsdp', axis=0, tiled=True)]
    pallas_call x0 -> x2, Pallas kernels: none -> 252 us  [the longest x1 159 us: reduce_scatter(): pl.pallas_call(functools.partial(rs_kernel, spread), out_shape=out, in_sp...]
    unnamed x2 -> x0, blocking collectives: 85.9 us -> none
    dot_general x36 -> x17, matrix products: 216 us -> 144 us  [the longest x12 86.6 us: mm(): lax.dot_general(a, b, (((ca,), (cb,)), ((), ())), preferred_element_type=...]
    unnamed x187 -> x101, local copies, waits for them, and re-layouts: 26.6 us -> 6.03 us
    another operation x7 -> x24, local copies, waits for them, and re-layouts: 0.53 us -> 17.8 us  [the longest x1 9.41 us: compute(): dqkv = jnp.stack([dq, dk, dv], axis=2).reshape(2 * rows, 3 * d).astype(BF)]
    sub x0 -> x1, matrix products: none -> 16.1 us  [compute(): prob = jax.nn.softmax(s, axis=-1)]
  transfers between devices with their start and end apart: 16 -> 0, of which waited for: 14 -> 0; matrix products, arithmetic and copies ran while one was open for 19% -> 0% of each run, Pallas kernels for 0% -> 0%
where the time goes in v1:
time: 519 us; the launch traced here: 514 us
  Pallas kernels  252 us (49%)
  matrix products  160 us (31%)
  local copies, waits for them, and re-layouts  56.8 us (11%)
  other arithmetic  43.4 us (8%)
    pallas_call x1, Pallas kernels, reduce_scatter(): pl.pallas_call(functools.partial(rs_kernel, spread), out_shape=out, in_sp...  159 us
    pallas_call x1, Pallas kernels, all_gather(): pl.pallas_call(functools.partial(ag_kernel, spread), out_shape=out, in_sp...  93 us
    dot_general x12, matrix products, mm(): lax.dot_general(a, b, (((ca,), (cb,)), ((), ())), preferred_element_type=...  86.6 us
    convert_element_type x1, other arithmetic, compute(): ds = (prob * (dp - jnp.sum(prob * dp, axis=-1, keepdims=True))).astype(BF)  21.2 us
    dot_general x1, matrix products, compute(): dp = jnp.einsum('gqhd,gkhd->ghqk', do, v, preferred_element_type=F32)  16.7 us
    sub x1, matrix products, compute(): prob = jax.nn.softmax(s, axis=-1)  16.1 us
    dot_general x1, matrix products, compute(): dv = jnp.einsum('ghqk,gqhd->gkhd', pb, do, preferred_element_type=F32)  13.9 us
    dot_general x1, matrix products, compute(): jnp.einsum('ghqk,gkhd->gqhd', pb, v, preferred_element_type=F32).astype(BF)  10.9 us

profile of v1, /device:TPU:0, one launch (start us, length us, event | category | flops | bytes accessed | tf_op | source)
XLA Modules:
  0.0 514.0 jit_solution(924797604588454239)
XLA Ops:
  7.0 2.4 dynamic-slice_bitcast_fusion
  9.4 93.0 %gather.1 = (bf16[512,768]{1,0:T(8,128)(2,1)S(1)}, bf16[512,768]{1,0:T(8,128)(2,1)S(1)}, f32[8,512]{1,0:T(8,128)S(1)}, bf16[768,2304]{1,0:T(8,128)(2,1)}, bf16[7...) custom-call(bf16[2,512,768]{2,1,0:T(8,128)(2,1)S(1)} %copy-done.2, ...), custom_call_target="tpu_custom_call" | custom-call | tf_op jit(solution)/shard_map/gather/pallas_call | solution.py:241
  104.2 2.3 sqrt_select_fusion
  106.5 8.8 %convolution_convert_fusion = bf16[1024,2304]{1,0:T(8,128)(2,1)} fusion(bf16[768,2304]{1,0:T(8,128)(2,1)} %get-tuple-element.30, f32[768]{0:T(1024)S(1)} %add.202, f32[768]{0:T(1024)S(1)} %mul.230, f32[1024]{0:T(1024)S(1)} %add_rsqrt_fusion.1, f32[1024]{0:T(1024)S(1)} %broadcast_multiply_fusion.5, bf16[512,768]{1,0:T(8,128)(2,1)S(1)} %get-tuple-element.28, ...), kind=kOutput, calls=%fused_computation.24 | convolution fusion | flops 3633315840 | bytes 9844736 | tf_op jit(solution)/shard_map/dot_general | solution.py:494
  115.3 6.6 %copy.67 = bf16[1024,2304]{0,1:T(8,128)(2,1)} copy(bf16[1024,2304]{1,0:T(8,128)(2,1)} %convolution_convert_fusion) | data formatting | bytes 9437184 | tf_op jit(solution)/shard_map/convert_element_type | solution.py:511
  121.9 8.8 %reshape.268 = bf16[2,512,3,12,64]{1,0,4,3,2:T(2,128)(2,1)} reshape(bf16[1024,2304]{0,1:T(8,128)(2,1)} %copy.67) | data formatting | bytes 9437184 | tf_op jit(solution)/shard_map/reshape | solution.py:512
  130.7 6.7 %fusion.65 = (bf16[2,512,1,12,64]{1,0,4,3,2:T(2,128)(2,1)S(1)}, bf16[2,512,1,12,64]{1,0,4,3,2:T(2,128)(2,1)}, bf16[2,512,1,12,64]{1,0,4,3,2:T(2,128)(2,1)}) fusion(bf16[2,512,3,12,64]{1,0,4,3,2:T(2,128)(2,1)} %reshape.268), kind=kLoop, calls=%fused_computation.151 | loop fusion | bytes 9437184 | tf_op jit(solution)/shard_map/slice | solution.py:513
  137.4 16.1 %fusion.67 = (f32[2,12,512]{2,1,0:T(8,128)S(1)}, f32[2,12,512,512]{2,3,1,0:T(8,128)}) fusion(f32[2,512,512]{1,2,0:T(8,128)} %sqrt_select_fusion, f32[12]{0:T(128)S(1)} %multiply_exponential_fusion, bf16[2,512,1,12,64]{1,0,4,3,2:T(2,128)(2,1)} %get-tuple-element.60, bf16[2,512,1,12,64]{1,0,4,3,2:T(2,128)(2,1)S(1)} %get-tuple-element.59), kind=kOutput, calls=%fused_computation.153 | convolution fusion | flops 836764160 | bytes 30457904 | tf_op jit(solution)/shard_map/sub | solution.py:518
  153.6 10.9 %fusion.43 = bf16[2,512,12,64]{1,3,2,0:T(8,128)(2,1)S(1)} fusion(bf16[2,512,1,12,64]{1,0,4,3,2:T(2,128)(2,1)} %get-tuple-element.61, f32[2,12,512,512]{2,3,1,0:T(8,128)} %get-tuple-element.91, f32[2,12,512]{2,1,0:T(8,128)S(1)} %get-tuple-element.90), kind=kOutput, calls=%fused_computation.77 | convolution fusion | flops 818675712 | bytes 28360704 | tf_op jit(solution)/shard_map/ghqk,gkhd->gqhd/dot_general | solution.py:520
  170.2 11.4 %multiply_convert_fusion.1 = (bf16[1024,3072]{1,0:T(8,128)(2,1)}, f32[1024,3072]{1,0:T(8,128)}) fusion(f32[3072]{0:T(1024)S(1)} %add.215, bf16[768,3072]{1,0:T(8,128)(2,1)S(1)} %bitcast.158, f32[1024,768]{1,0:T(8,128)S(1)} %get-tuple-element.93, f32[768]{0:T(1024)S(1)} %add.212, f32[768]{0:T(1024)S(1)} %mul.241, f32[1024]{0:T(1024)S(1)} %add_rsqrt_fusion, ...), kind=kOutput, calls=%fused_computation.14 | convolution fusion | flops 4854644736 | bytes 26765312 | tf_op jit(solution)/shard_map/dot_general | solution.py:494
  181.6 15.6 %convert_reduce_fusion = (f32[3072]{0:T(1024)S(1)}, bf16[1024,3072]{1,0:T(8,128)(2,1)S(1)}) fusion(f32[1024,3072]{1,0:T(8,128)} %get-tuple-element.98, f32[3072]{0:T(1024)S(1)} %add.215, bf16[3072,768]{1,0:T(8,128)(2,1)S(1)} %bitcast.160, f32[1024]{0:T(1024)S(1)} %bitcast.143, bf16[512,768]{1,0:T(8,128)(2,1)S(1)} %get-tuple-element.35, ...), kind=kOutput, calls=%fused_computation.13 | convolution fusion | flops 4877448192 | bytes 25194496 | tf_op jit(solution)/shard_map/dot_general | solution.py:494
  197.3 10.3 %add_convert_fusion = bf16[1024,768]{1,0:T(8,128)(2,1)} fusion(f32[1024,768]{1,0:T(8,128)S(1)} %get-tuple-element.93, bf16[1024,3072]{1,0:T(8,128)(2,1)} %get-tuple-element.97, bf16[3072,768]{1,0:T(8,128)(2,1)S(1)} %bitcast.160, f32[768]{0:T(1024)S(1)} %add.220), kind=kOutput, calls=%fused_computation.57 | convolution fusion | flops 4834197504 | bytes 15731712 | tf_op jit(solution)/shard_map/dot_general | solution.py:494
  207.6 7.7 %convolution_convert_fusion.1.refs_3_ = bf16[3072,768]{1,0:T(8,128)(2,1)} fusion(bf16[1024,3072]{1,0:T(8,128)(2,1)S(1)} %copy-done.42, f32[1024]{0:T(1024)S(1)} %bitcast.144, bf16[512,768]{1,0:T(8,128)(2,1)S(1)} %get-tuple-element.35, bf16[512,768]{1,0:T(8,128)(2,1)S(1)} %copy-done.20), kind=kOutput, calls=%fused_computation.25 | convolution fusion | flops 4838916096 | bytes 12587008 | tf_op jit(solution)/shard_map/dot_general | solution.py:494
  215.2 7.2 %multiply_reduce_fusion.1 = (f32[768]{0:T(1024)S(1)}, f32[1024]{0:T(1024)S(1)}, f32[1024]{0:T(1024)S(1)}, f32[768]{0:T(1024)S(1)}, f32[1024,768]{1,0:T(8,128)}) fusion(f32[1024,768]{1,0:T(8,128)S(1)} %get-tuple-element.93, f32[1024]{0:T(1024)S(1)} %add_rsqrt_fusion, f32[1024]{0:T(1024)S(1)} %broadcast_multiply_fusion.4, f32[768]{0:T(1024)S(1)} %mul.241, ...), kind=kOutput, calls=%fused_computation.49 | convolution fusion | flops 4838912000 | bytes 17327104 | tf_op jit(solution)/shard_map/dot_general | solution.py:494
  222.4 2.5 slice_bitcast_fusion.1
  225.0 4.6 convert_reduce_fusion.3
  229.6 8.0 %convolution_convert_fusion.2.refs_2_ = bf16[768,3072]{1,0:T(8,128)(2,1)} fusion(bf16[1024,3072]{1,0:T(8,128)(2,1)S(1)} %copy-done.41, f32[1024,768]{1,0:T(8,128)S(1)} %copy-done.10, f32[768]{0:T(1024)S(1)} %add.212, f32[768]{0:T(1024)S(1)} %mul.241, f32[1024]{0:T(1024)S(1)} %add_rsqrt_fusion, f32[1024]{0:T(1024)S(1)} %broadcast_multiply_fusion.4), kind=kOutput, calls=%fused_computation.26 | convolution fusion | flops 4838129664 | bytes 14170112 | tf_op jit(solution)/shard_map/dot_general | solution.py:494
  237.6 2.5 convolution_convert_fusion.5.refs_1_
  240.1 2.6 convolution_convert_fusion.4
  244.4 2.4 reshape.270
  246.8 13.9 %fusion.40 = bf16[2,512,1,12,64]{1,4,3,0,2:T(8,128)(2,1)} fusion(bf16[2,512,12,64]{1,0,3,2:T(2,128)(2,1)} %reshape.270, f32[2,12,512,512]{2,3,1,0:T(8,128)} %get-tuple-element.91, f32[2,12,512]{2,1,0:T(8,128)S(1)} %get-tuple-element.90), kind=kOutput, calls=%fused_computation.76 | convolution fusion | flops 818675712 | bytes 28360704 | tf_op jit(solution)/shard_map/ghqk,gqhd->gkhd/dot_general | solution.py:542
  260.7 16.7 %multiply_reduce_fusion = (f32[2,12,512]{2,1,0:T(8,128)S(1)}, f32[2,12,512,512]{2,3,1,0:T(8,128)}) fusion(f32[2,12,512,512]{2,3,1,0:T(8,128)} %get-tuple-element.91, f32[2,12,512]{2,1,0:T(8,128)S(1)} %get-tuple-element.90, bf16[2,512,1,12,64]{1,0,4,3,2:T(2,128)(2,1)S(1)} %copy-done.21, bf16[2,512,12,64]{1,0,3,2:T(2,128)(2,1)} %reshape.270), kind=kOutput, calls=%fused_computation.2 | convolution fusion | flops 824168448 | bytes 53575680 | tf_op jit(solution)/shard_map/gqhd,gkhd->ghqk/dot_general | solution.py:543
  277.3 21.2 %multiply_convert_fusion = bf16[2,12,512,512]{2,3,1,0:T(8,128)(2,1)} fusion(f32[2,12,512,512]{2,3,1,0:T(8,128)} %get-tuple-element.96, f32[2,12,512]{2,1,0:T(8,128)S(1)} %get-tuple-element.95, f32[2,12,512,512]{2,3,1,0:T(8,128)} %get-tuple-element.91, f32[2,12,512]{2,1,0:T(8,128)S(1)} %get-tuple-element.90), kind=kLoop, calls=%fused_computation.1 | loop fusion | flops 25165824 | bytes 63012864 | tf_op jit(solution)/shard_map/convert_element_type | solution.py:544
  298.5 8.6 %fusion.47 = bf16[2,512,1,12,64]{1,4,3,0,2:T(8,128)(2,1)S(1)} fusion(bf16[2,12,512,512]{2,3,1,0:T(8,128)(2,1)} %multiply_convert_fusion, bf16[2,512,1,12,64]{1,0,4,3,2:T(2,128)(2,1)S(1)} %copy-done.19), kind=kOutput, calls=%fused_computation.79 | convolution fusion | flops 806879232 | bytes 15728640 | tf_op jit(solution)/shard_map/ghqk,gqhd->gkhd/dot_general | solution.py:546
  307.2 6.8 %fusion.46 = bf16[2,512,1,12,64]{1,4,3,0,2:T(8,128)(2,1)S(1)} fusion(bf16[2,12,512,512]{2,3,1,0:T(8,128)(2,1)} %multiply_convert_fusion, bf16[2,512,1,12,64]{1,0,4,3,2:T(2,128)(2,1)S(1)} %copy-done.18), kind=kOutput, calls=%fused_computation.78 | convolution fusion | flops 806879232 | bytes 15728640 | tf_op jit(solution)/shard_map/ghqk,gkhd->gqhd/dot_general | solution.py:545
  314.0 2.6 pad_maximum_fusion
  316.6 9.4 %copy.80 = bf16[2,512,3,12,64]{1,0,4,3,2:T(2,128)(2,1)} copy(bf16[2,512,3,12,64]{1,4,3,0,2:T(8,128)(2,1)} %pad_maximum_fusion) | data formatting | bytes 9437184 | tf_op jit(solution)/shard_map/stack | solution.py:547
  326.1 4.0 copy.94
  330.2 4.7 fusion.26
  334.9 6.3 %convolution_convert_fusion.3.refs_0_ = bf16[768,2304]{1,0:T(8,128)(2,1)} fusion(bf16[1024,2304]{0,1:T(8,128)(2,1)S(1)} %bitcast.135, f32[768]{0:T(1024)S(1)} %copy-done.38, f32[768]{0:T(1024)S(1)} %copy-done.34, f32[1024]{0:T(1024)S(1)} %copy-done.36, f32[1024]{0:T(1024)S(1)} %copy-done.32, bf16[512,768]{1,0:T(8,128)(2,1)S(1)} %copy-done.1, ...), kind=kOutput, calls=%fused_computation.27 | convolution fusion | flops 3632726016 | bytes 9844736 | tf_op jit(solution)/shard_map/dot_general | solution.py:494
  344.8 159.4 %scatter.1 = (bf16[2,24,2304]{2,1,0:T(8,128)(2,1)}, bf16[2,24,768]{2,1,0:T(8,128)(2,1)}, bf16[2,24,3072]{2,1,0:T(8,128)(2,1)}, bf16[2,96,768]{2,1,0:T(8,128)(2,1...) custom-call(bf16[768,2304]{1,0:T(8,128)(2,1)} %convolution_convert_fusion.3.refs_0_, ...), custom_call_target="tpu_custom_call" | custom-call | tf_op jit(solution)/shard_map/scatter/pallas_call | solution.py:447
  504.3 2.9 maximum_select_fusion
  (172 shorter events, 25.3 us)
Async XLA Ops:
  0.6 8.7 %copy-start.2 = (bf16[2,512,768]{2,1,0:T(8,128)(2,1)S(1)}, bf16[2,512,768]{2,1,0:T(8,128)(2,1)}, u32[]{:S(2)}) copy-start(bf16[2,512,768]{2,1,0:T(8,128)(2,1)} %refs_0_.1) | copy-start | bytes 4718596
  0.7 8.7 %copy-start.3 = (bf16[2,24,3072]{2,1,0:T(8,128)(2,1)S(1)}, bf16[2,24,3072]{2,1,0:T(8,128)(2,1)}, u32[]{:S(2)}) copy-start(bf16[2,24,3072]{2,1,0:T(8,128)(2,1)} %refs_5_.1) | copy-start | bytes 884740
  0.7 8.7 %copy-start.6 = (bf16[2,24,768]{2,1,0:T(8,128)(2,1)S(1)}, bf16[2,24,768]{2,1,0:T(8,128)(2,1)}, u32[]{:S(2)}) copy-start(bf16[2,24,768]{2,1,0:T(8,128)(2,1)} %refs_4_.1) | copy-start | bytes 221188
  9.3 94.0 %copy-start.11 = (bf16[512,768]{1,0:T(8,128)(2,1)}, bf16[512,768]{1,0:T(8,128)(2,1)S(1)}, u32[]{:S(2)}) copy-start(bf16[512,768]{1,0:T(8,128)(2,1)S(1)} %get-tuple-element.103) | copy-start | bytes 2359300
  102.4 64.3 %copy-start = (bf16[512,768]{1,0:T(8,128)(2,1)}, bf16[512,768]{1,0:T(8,128)(2,1)S(1)}, u32[]{:S(2)}) copy-start(bf16[512,768]{1,0:T(8,128)(2,1)S(1)} %get-tuple-element.28) | copy-start | bytes 2359300
  102.7 12.6 %copy-start.31 = (f32[1024]{0:T(1024)}, f32[1024]{0:T(1024)S(1)}, u32[]{:S(2)}) copy-start(f32[1024]{0:T(1024)S(1)} %broadcast_multiply_fusion.5) | copy-start | bytes 12292
  103.4 11.9 %copy-start.35 = (f32[1024]{0:T(1024)}, f32[1024]{0:T(1024)S(1)}, u32[]{:S(2)}) copy-start(f32[1024]{0:T(1024)S(1)} %add_rsqrt_fusion.1) | copy-start | bytes 12292
  103.9 11.4 %copy-start.33 = (f32[768]{0:T(1024)}, f32[768]{0:T(1024)S(1)}, u32[]{:S(2)}) copy-start(f32[768]{0:T(1024)S(1)} %mul.230) | copy-start | bytes 9220
  104.1 11.2 %copy-start.37 = (f32[768]{0:T(1024)}, f32[768]{0:T(1024)S(1)}, u32[]{:S(2)}) copy-start(f32[768]{0:T(1024)S(1)} %add.202) | copy-start | bytes 9220
  137.4 16.1 %copy-start.17 = (bf16[2,512,1,12,64]{1,0,4,3,2:T(2,128)(2,1)}, bf16[2,512,1,12,64]{1,0,4,3,2:T(2,128)(2,1)S(1)}, u32[]{:S(2)}) copy-start(bf16[2,512,1,12,64]{1,0,4,3,2:T(2,128)(2,1)S(1)} %get-tuple-element.59) | copy-start | bytes 4718596
  168.3 46.9 %copy-start.9 = (f32[1024,768]{1,0:T(8,128)}, f32[1024,768]{1,0:T(8,128)S(1)}, u32[]{:S(2)}) copy-start(f32[1024,768]{1,0:T(8,128)S(1)} %get-tuple-element.93) | copy-start | bytes 9437188
  168.3 13.2 %slice-start.2 = ((s8[4718592]{0:T(1024)(128)(4,1)}), s8[4194304]{0:T(1024)(128)(4,1)S(1)}, s32[]{:S(2)}) async-start(s8[4718592]{0:T(1024)(128)(4,1)} %bitcast.159), calls=%async_computation.2 | async-start | bytes 8388608
  170.2 11.4 %copy-start.20 = (bf16[512,768]{1,0:T(8,128)(2,1)S(1)}, bf16[512,768]{1,0:T(8,128)(2,1)}, u32[]{:S(2)}) copy-start(bf16[512,768]{1,0:T(8,128)(2,1)} %get-tuple-element.102) | copy-start | bytes 2359300
  170.2 11.4 %slice-start.3 = ((s8[4718592]{0:T(1024)(128)(4,1)}), s8[524288]{0:T(1024)(128)(4,1)S(1)}, s32[]{:S(2)}) async-start(s8[4718592]{0:T(1024)(128)(4,1)} %bitcast.159), calls=%async_computation.3 | async-start | bytes 1048576
  197.2 18.0 %copy-start.40 = (bf16[1024,3072]{1,0:T(8,128)(2,1)}, bf16[1024,3072]{1,0:T(8,128)(2,1)S(1)}, u32[]{:S(2)}) copy-start(bf16[1024,3072]{1,0:T(8,128)(2,1)S(1)} %get-tuple-element.101) | copy-start | bytes 18874372
  197.2 10.3 %copy-start.42 = (bf16[1024,3072]{1,0:T(8,128)(2,1)S(1)}, bf16[1024,3072]{1,0:T(8,128)(2,1)}, u32[]{:S(2)}) copy-start(bf16[1024,3072]{1,0:T(8,128)(2,1)} %get-tuple-element.97) | copy-start | bytes 18874372
  224.9 4.6 copy-start.41
  229.6 10.5 %copy-start.15 = (f32[1024,768]{1,0:T(8,128)}, f32[1024,768]{1,0:T(8,128)S(1)}, u32[]{:S(2)}) copy-start(f32[1024,768]{1,0:T(8,128)S(1)} %get-tuple-element.56) | copy-start | bytes 9437188
  229.6 8.0 %copy-start.24 = (bf16[96,8,2,512]{3,1,2,0:T(8,128)(2,1)S(1)}, bf16[96,8,2,512]{3,1,2,0:T(8,128)(2,1)}, u32[]{:S(2)}) copy-start(bf16[96,8,2,512]{3,1,2,0:T(8,128)(2,1)} %copy-done.23) | copy-start | bytes 4718596
  246.8 13.9 %copy-start.21 = (bf16[2,512,1,12,64]{1,0,4,3,2:T(2,128)(2,1)S(1)}, bf16[2,512,1,12,64]{1,0,4,3,2:T(2,128)(2,1)}, u32[]{:S(2)}) copy-start(bf16[2,512,1,12,64]{1,0,4,3,2:T(2,128)(2,1)} %get-tuple-element.61) | copy-start | bytes 4718596
  277.3 21.2 %copy-start.19 = (bf16[2,512,1,12,64]{1,0,4,3,2:T(2,128)(2,1)S(1)}, bf16[2,512,1,12,64]{1,0,4,3,2:T(2,128)(2,1)}, u32[]{:S(2)}) copy-start(bf16[2,512,1,12,64]{1,0,4,3,2:T(2,128)(2,1)} %get-tuple-element.60) | copy-start | bytes 4718596
  298.5 8.6 %copy-start.18 = (bf16[2,512,1,12,64]{1,0,4,3,2:T(2,128)(2,1)S(1)}, bf16[2,512,1,12,64]{1,0,4,3,2:T(2,128)(2,1)}, u32[]{:S(2)}) copy-start(bf16[2,512,1,12,64]{1,0,4,3,2:T(2,128)(2,1)} %copy-done.17) | copy-start | bytes 4718596
  307.1 6.9 %copy-start.22 = (bf16[2,512,1,12,64]{1,4,3,0,2:T(8,128)(2,1)S(1)}, bf16[2,512,1,12,64]{1,4,3,0,2:T(8,128)(2,1)}, u32[]{:S(2)}) copy-start(bf16[2,512,1,12,64]{1,4,3,0,2:T(8,128)(2,1)} %fusion.40) | copy-start | bytes 4718596
  326.0 4.1 copy-start.36
  326.0 4.1 copy-start.39
  330.1 4.7 copy-start.38
  334.9 6.3 %copy-start.16 = (f32[1024,768]{1,0:T(8,128)S(1)}, f32[1024,768]{1,0:T(8,128)}, u32[]{:S(2)}) copy-start(f32[1024,768]{1,0:T(8,128)} %copy-done.15) | copy-start | bytes 9437188
  504.2 4.3 copy-start.29
  504.2 5.0 copy-start.28
  504.2 5.8 %copy-start.27 = (bf16[2,24,3072]{2,1,0:T(8,128)(2,1)S(1)}, bf16[2,24,3072]{2,1,0:T(8,128)(2,1)}, u32[]{:S(2)}) copy-start(bf16[2,24,3072]{2,1,0:T(8,128)(2,1)} %get-tuple-element.41) | copy-start | bytes 884740
  504.3 6.6 %copy-start.26 = (bf16[2,96,768]{2,1,0:T(8,128)(2,1)S(1)}, bf16[2,96,768]{2,1,0:T(8,128)(2,1)}, u32[]{:S(2)}) copy-start(bf16[2,96,768]{2,1,0:T(8,128)(2,1)} %get-tuple-element.42) | copy-start | bytes 884740
  504.3 7.5 %copy-start.25 = (bf16[512,768]{1,0:T(8,128)(2,1)S(1)}, bf16[512,768]{1,0:T(8,128)(2,1)}, u32[]{:S(2)}) copy-start(bf16[512,768]{1,0:T(8,128)(2,1)} %get-tuple-element.37) | copy-start | bytes 2359300
  (15 other events, 46.1 us)
